TPU v7x, 32 devices: a whole 2x2x4 slice. The times are simulated.
32 devices in a mesh: groups: 2 (over x), inst: 4 (over y, core), tp: 4 (over z).
Axes of the slice: x: 2, y: 2, z: 4, core: 2. Of those that a mesh axis runs over, the one named last changes fastest.
Arguments:
- queries: bfloat16 [512, 8192], P(('groups', 'inst'), 'tp'), parts along dimension 0, may hold values from -40 to 40
- k_pool: bfloat16 [1024, 8, 128, 128], P(('groups', 'inst'), 'tp'), parts along dimension 0, may hold values from -6 to 6
- v_pool: bfloat16 [1024, 8, 128, 128], P(('groups', 'inst'), 'tp'), parts along dimension 0, may hold values from -6 to 6
- out_weight: bfloat16 [8192, 4096], P('tp'), may hold values from -0.5 to 0.5
- lengths: int32 [8, 32], P(('groups', 'inst')), parts along dimension 0, may hold values from 1 to 512, 8192 in all within a row
- block_table: int32 [8, 128], P(('groups', 'inst')), parts along dimension 0, may hold values from 0 to 127, each once within a row
- routes: int32 [256, 1], P(('groups', 'inst')), parts along dimension 0, may hold values from 0 to 3; in each aligned block of 32 rows (0 to 31, 32 to 63, ...) at most 16 rows name the same one
Outputs:
- attended: bfloat16 [512, 4096], P(('groups', 'inst')), parts along dimension 0
There are 2 independent parts, one for each index of `groups`. A program takes and returns all parts, laid end to end along the dimension named above; an argument that names none is the same for every part. Nothing has to cross between parts.
Inputs may be any that keep to these rules, and one draw needn't show every extreme that they name: `routes`: in the rows of one instance no target is named more than 16 times, a bound that some block reaches. The 32 lengths of each instance sum to 8192, and the largest is 512. `block_table`: each instance's row names each of its 128 pool blocks once.
All inputs are finite; a program needn't handle non-finite values.
Results may differ from a plain program's by a relative error of at most 0.0058.
Values may be sent and summed in bfloat16 or wider, within the bound.
A program may use at most 192 MiB of HBM per device.

v0:
```python
import math

import jax
import jax.numpy as jnp
from jax import lax
from jax.sharding import PartitionSpec as P


def attend(query, key_rows, value_rows, ctx_len):
    slots = query.shape[0]
    head_dim = key_rows.shape[4]
    grouped = query.reshape(slots, key_rows.shape[2], -1, head_dim)
    scores = jnp.einsum(
        "skgd,smkbd->skgmb", grouped, key_rows, preferred_element_type=jnp.float32
    ) / math.sqrt(head_dim)
    position = jnp.arange(key_rows.shape[1] * key_rows.shape[3], dtype=jnp.int32).reshape(
        key_rows.shape[1], key_rows.shape[3]
    )
    visible = (position[None] < ctx_len[:, None, None])[:, None, None]
    scores = jnp.where(visible, scores, -1e30)
    peak = jnp.max(scores, axis=(3, 4), keepdims=True)
    scaled = jnp.exp(scores - peak)
    weights = (scaled / jnp.sum(scaled, axis=(3, 4), keepdims=True)).astype(jnp.bfloat16)
    mixed = jnp.einsum(
        "skgmb,smkbd->skgd", weights, value_rows, preferred_element_type=jnp.float32
    ).astype(jnp.bfloat16)
    mixed = jnp.where((ctx_len > 0)[:, None, None, None], mixed, jnp.zeros_like(mixed))
    return mixed.reshape(slots, -1)


def local_slots(routes, lengths, block_table, num_inst, slot_count):
    target = routes[:, 0]
    row_count = target.shape[0]
    capacity = slot_count // num_inst
    onehot = (target[:, None] == jnp.arange(num_inst, dtype=jnp.int32)[None, :]).astype(jnp.int32)
    before = jnp.cumsum(onehot, axis=0) - onehot
    rank_in = jnp.sum(before * onehot, axis=1)
    slot_index = target * capacity + rank_in
    matches = (slot_index[:, None] == jnp.arange(slot_count, dtype=jnp.int32)[None, :]).astype(
        jnp.int32
    )
    row_of = jnp.sum(matches * jnp.arange(row_count, dtype=jnp.int32)[:, None], axis=0)
    filled = jnp.sum(matches, axis=0) > 0
    ctx_len = jnp.where(filled, lengths[0][row_of], 0)
    block_ids = block_table.reshape(row_count, -1)[row_of]
    return (block_ids, ctx_len)


def local(queries, k_pool, v_pool, out_weight, lengths, block_table, routes):
    num_inst = lax.axis_size("inst")
    slot_count = queries.shape[0]
    capacity = slot_count // num_inst
    block_ids, ctx_len = local_slots(routes, lengths, block_table, num_inst, slot_count)
    key_rows = k_pool[block_ids]
    value_rows = v_pool[block_ids]
    remote_query = lax.all_to_all(
        queries.reshape(num_inst, capacity, -1), "inst", split_axis=0, concat_axis=0, tiled=True
    )
    source_out = attend(remote_query.reshape(slot_count, -1), key_rows, value_rows, ctx_len)
    head_out = lax.all_to_all(
        source_out.reshape(num_inst, capacity, -1), "inst", split_axis=0, concat_axis=0, tiled=True
    ).reshape(slot_count, -1)
    partial_value = jnp.dot(head_out, out_weight, preferred_element_type=jnp.float32)
    return lax.psum(partial_value, "tp").astype(jnp.bfloat16)


def solution(mesh):
    return jax.shard_map(
        local,
        mesh=mesh,
        in_specs=(
            P(("groups", "inst"), "tp"),
            P(("groups", "inst"), "tp", None, None),
            P(("groups", "inst"), "tp", None, None),
            P("tp", None),
            P(("groups", "inst"), None),
            P(("groups", "inst"), None),
            P(("groups", "inst"), None),
        ),
        out_specs=P(("groups", "inst"), None),
        check_vma=False,
    )
```

profile of v0, /device:TPU:0, one launch (start us, length us, event | category | flops | bytes accessed | tf_op | source)
XLA Modules:
  0.0 115.7 jit_solution(18167128931159352288)
XLA Ops:
  0.0 0.0 copy-start
  0.0 4.4 %all-to-all-start = ((bf16[4,16,2048]{2,1,0:T(8,128)(2,1)}), bf16[4,16,2048]{2,1,0:T(8,128)(2,1)S(1)}, u32[]{:S(2)}, u32[]{:S(2)}) async-start(bf16[4,16,2048]{2,1,0:T(8,128)(2,1)} %bitcast.56), calls=%async_computation | async-start | bytes 524288 | tf_op jit(solution)/shard_map/all_to_all | solution.py:56
  4.4 0.7 fusion.21
  5.1 0.1 reduce_window_sum.11
  5.2 0.8 select_reduce_fusion.1
  6.0 0.7 fusion.23
  6.7 0.1 convert_reduce_fusion
  6.8 0.5 broadcast.121
  7.3 1.3 %reduce.3 = s32[128]{0:T(128)S(1)} reduce(s32[1,128]{1,0:T(1,128)} %param.12, s32[]{:T(128)} %broadcast.121), dimensions={0}, to_apply=%param.12.reduce_sub_computation.3 | reduce | bytes 1028 | tf_op args[5]
  8.6 0.1 reshape.62
  8.7 0.0 copy-done
  8.7 0.8 gather_fusion
  9.5 0.6 gather_fusion.1
  10.1 0.1 reshape.83
  10.2 12.9 %gather_fusion.2 = bf16[256,2,128,128]{3,2,1,0:T(8,128)(2,1)} fusion(bf16[128,2,128,128]{3,2,1,0:T(8,128)(2,1)} %param.8, s32[1024]{0:T(1024)S(1)} %pad_clamp_fusion), kind=kCustom, calls=%fused_computation.2 | custom fusion | bytes 33555456 | tf_op jit(solution)/shard_map/gather | solution.py:54
  23.1 12.9 %gather_fusion.3 = bf16[256,2,128,128]{3,2,1,0:T(8,128)(2,1)} fusion(bf16[128,2,128,128]{3,2,1,0:T(8,128)(2,1)} %param.9, s32[1024]{0:T(1024)S(1)} %pad_clamp_fusion), kind=kCustom, calls=%fused_computation.3 | custom fusion | bytes 33555456 | tf_op jit(solution)/shard_map/gather | solution.py:55
  36.0 0.1 broadcast_compare_fusion
  36.1 0.0 all-to-all-done
  36.2 8.2 %bitcast_reduce_fusion = (f32[64,2,8]{2,1,0:T(2,128)S(1)}, f32[64,2,4,128,8]{3,4,2,1,0:T(8,128)S(1)}) fusion(pred[64,4,128]{2,1,0:T(4,128)(4,1)S(1)} %broadcast_compare_fusion, bf16[64,2,8,128,1]{3,2,1,0,4:T(8,128)(2,1)S(1)} %bitcast.57, bf16[64,4,2,128,128]{4,3,2,1,0:T(8,128)(2,1)} %bitcast.53), kind=kOutput, calls=%fused_computation.9 | convolution fusion | flops 135789568 | bytes 19173376 | tf_op jit(solution)/shard_map/skgd,smkbd->skgmb/dot_general | solution.py:13
  44.4 0.9 fusion.5
  45.2 7.3 %fusion.12 = bf16[64,2,8,128]{3,2,1,0:T(8,128)(2,1)S(1)} fusion(bf16[64,4,2,128,128]{4,3,2,1,0:T(8,128)(2,1)} %bitcast.52, f32[64,2,4,128,8]{3,4,2,1,0:T(8,128)S(1)} %get-tuple-element.10, f32[64,2,8]{2,1,0:T(2,128)S(1)} %fusion.5, f32[64,2,8]{2,1,0:T(2,128)S(1)} %get-tuple-element.9, pred[64,4,128]{2,1,0:T(4,128)(4,1)S(1)} %broadcast_compare_fusion, ...), kind=kOutput, calls=%fused_computation.16 | convolution fusion | flops 137101312 | bytes 19177536 | tf_op jit(solution)/shard_map/skgmb,smkbd->skgd/dot_general | solution.py:24
  52.5 0.1 reshape_reshape.7
  52.6 9.3 %all_to_all.10 = bf16[4,16,2048]{2,1,0:T(8,128)(2,1)S(1)} all-to-all(bf16[4,16,2048]{2,1,0:T(8,128)(2,1)S(1)} %reshape_reshape.7), channel_id=1, replica_groups=mesh['groups'=2,'inst'=4,'tp'=4] {'inst'}, dimensions={0} | all-to-all | bytes 524288 | tf_op jit(solution)/shard_map/all_to_all | solution.py:60
  61.9 0.0 copy-start.1
  61.9 8.8 %fusion.26 = f32[64,4096]{1,0:T(8,128)S(1)} fusion(bf16[64,2048]{1,0:T(8,128)(2,1)S(1)} %bitcast.54, bf16[2048,4096]{1,0:T(8,128)(2,1)} %param.10), kind=kOutput, calls=%fused_computation.42 | convolution fusion | flops 1073741824 | bytes 18087936 | tf_op jit(solution)/shard_map/dot_general | solution.py:63
  70.7 44.9 %all-reduce.1 = bf16[64,4096]{1,0:T(8,128)(2,1)} all-reduce(f32[64,4096]{1,0:T(8,128)S(1)} %fusion.26), channel_id=1, replica_groups=mesh['groups'=2,'inst'=4,'tp'=4] {'tp'}, use_global_device_ids=true, to_apply=%region_6.7 | all-reduce | flops 262144 | bytes 1572864 | tf_op jit(solution)/shard_map/psum | solution.py:64
  115.7 0.0 copy-done.1
  (7 shorter events, 0.1 us)
Async XLA Ops:
  0.0 8.7 %copy-start = (s32[1,32]{1,0:T(1,128)S(1)}, s32[1,32]{1,0:T(1,128)}, u32[]{:S(2)}) copy-start(s32[1,32]{1,0:T(1,128)} %param.11) | copy-start | bytes 388
  0.0 36.1 %all-to-all-start = ((bf16[4,16,2048]{2,1,0:T(8,128)(2,1)}), bf16[4,16,2048]{2,1,0:T(8,128)(2,1)S(1)}, u32[]{:S(2)}, u32[]{:S(2)}) async-start(bf16[4,16,2048]{2,1,0:T(8,128)(2,1)} %bitcast.56), calls=%async_computation | async-start | bytes 524288 | tf_op jit(solution)/shard_map/all_to_all | solution.py:56
  61.9 53.7 %copy-start.1 = (s32[1,32]{1,0:T(1,128)S(1)}, s32[1,32]{1,0:T(1,128)}, u32[]{:S(2)}) copy-start(s32[1,32]{1,0:T(1,128)} %param.11) | copy-start | bytes 388
where the time goes:
time: 116 us
  blocking collectives  54.2 us (47%)
  local copies, waits for them, and re-layouts  28 us (24%)
  matrix products  24.3 us (21%)
  other arithmetic  4.73 us (4%)
  starting transfers between devices  4.37 us (4%)
    psum x1, blocking collectives, local(): return lax.psum(partial_value, 'tp').astype(jnp.bfloat16)  44.9 us
    gather x1, local copies, waits for them, and re-layouts, local(): value_rows = v_pool[block_ids]  12.9 us
    gather x1, local copies, waits for them, and re-layouts, local(): key_rows = k_pool[block_ids]  12.9 us
    all_to_all x1, blocking collectives, local(): lax.all_to_all(source_out.reshape(num_inst, capacity, -1), 'inst', split_...  9.29 us
    dot_general x1, matrix products, local(): jnp.dot(head_out, out_weight, preferred_element_type=jnp.float32)  8.8 us
    dot_general x1, matrix products, attend(): jnp.einsum('skgd,smkbd->skgmb', grouped, key_rows, preferred_element_type...  8.18 us
    dot_general x1, matrix products, attend(): jnp.einsum('skgmb,smkbd->skgd', weights, value_rows, preferred_element_ty...  7.28 us
    all_to_all x1, starting transfers between devices, local(): lax.all_to_all(queries.reshape(num_inst, capacity, -1), 'inst', split_axi...  4.37 us
  transfers between devices with their start and end apart: 1, of which 0 were waited for; matrix products, arithmetic and copies ran while one was open for 27% of the time, Pallas kernels for 0%

commit v1 on v0

v1 whole, which is shorter than its diff:
```python
import functools
import math

import jax
import jax.numpy as jnp
from jax import lax
from jax.experimental import pallas as pl
from jax.experimental.pallas import tpu as pltpu
from jax.sharding import PartitionSpec as P

MESH = pl.DeviceIdType.MESH
F32 = jnp.float32
BF16 = jnp.bfloat16
PIECES = 4


def kernel(
    num_inst, num_tp, q_hbm, k_hbm, v_hbm, w_hbm, len_ref, table_ref, route_ref, out_ref,
    k_buf, v_buf, w_buf, q_in, q_heads, score, mixed, act, place_t, rs_send, rs_in, own, gathered, y_send,
    k_sem, v_sem, w_sem, q_own_sem, q_ssem, q_rsem, rs_ssem, rs_rsem, ag_ssem, ag_rsem, y_ssem, y_rsem,
):
    me = lax.axis_index("inst")
    tp = lax.axis_index("tp")
    blocks, kv_heads, block_len, head_dim = k_buf.shape
    cap = q_in.shape[1]
    cols = q_in.shape[2]
    rows = route_ref.shape[0]
    heads = cols // head_dim
    group = heads // kv_heads
    per_req = table_ref.shape[1] // rows
    chunk = w_buf.shape[2]

    def inst_peer(k):
        return lax.rem(me + k, num_inst)

    def tp_peer(k):
        return lax.rem(tp + k, num_tp)

    size = blocks // PIECES
    k_copies = [
        pltpu.make_async_copy(k_hbm.at[pl.ds(i * size, size)], k_buf.at[pl.ds(i * size, size)], k_sem.at[i])
        for i in range(PIECES)
    ]
    v_copies = [
        pltpu.make_async_copy(v_hbm.at[pl.ds(i * size, size)], v_buf.at[pl.ds(i * size, size)], v_sem.at[i])
        for i in range(PIECES)
    ]
    w_copies = []
    for i in range(num_tp):
        column = pl.multiple_of(tp_peer((i + 1) % num_tp) * chunk, 128)
        w_copies.append(pltpu.make_async_copy(w_hbm.at[:, pl.ds(column, chunk)], w_buf.at[i], w_sem.at[i]))
    q_own = pltpu.make_async_copy(q_hbm.at[me], q_in.at[me], q_own_sem)
    q_own.start()
    for c in k_copies + v_copies + w_copies:
        c.start()

    barrier = pltpu.get_barrier_semaphore()
    for k in range(1, num_inst):
        pl.semaphore_signal(barrier, inc=1, device_id={"inst": inst_peer(k)}, device_id_type=MESH)
    for k in range(1, num_tp):
        pl.semaphore_signal(barrier, inc=1, device_id={"tp": tp_peer(k)}, device_id_type=MESH)
    pl.semaphore_wait(barrier, num_inst + num_tp - 2)

    q_copies = []
    for k in range(1, num_inst):
        peer = inst_peer(k)
        c = pltpu.make_async_remote_copy(
            src_ref=q_hbm.at[peer], dst_ref=q_in.at[me], send_sem=q_ssem.at[k], recv_sem=q_rsem.at[me],
            device_id={"inst": peer}, device_id_type=MESH,
        )
        c.start()
        q_copies.append(c)

    target = route_ref[...]
    lane = lax.broadcasted_iota(jnp.int32, (rows, 128), 1)
    onehot = (target == lane).astype(F32)
    earlier = (
        lax.broadcasted_iota(jnp.int32, (rows, rows), 0) > lax.broadcasted_iota(jnp.int32, (rows, rows), 1)
    ).astype(F32)
    before = jnp.dot(earlier, onehot, preferred_element_type=F32)
    rank = jnp.sum(before * onehot, axis=1, keepdims=True).astype(jnp.int32)
    slot = target * cap + rank
    place = (slot == lane).astype(F32)
    turned = jnp.transpose(place)
    for t in range(num_inst):
        place_t[t] = turned[t * cap:(t + 1) * cap, :]

    q_own.wait()
    for k in range(1, num_inst):
        src = inst_peer(k)
        pltpu.make_async_remote_copy(
            src_ref=q_hbm.at[src], dst_ref=q_in.at[src], send_sem=q_ssem.at[k], recv_sem=q_rsem.at[src],
            device_id={"inst": src}, device_id_type=MESH,
        ).wait_recv()
    total = jnp.zeros((rows, cols), F32)
    for t in range(num_inst):
        here = (slot - t * cap == lax.broadcasted_iota(jnp.int32, (rows, cap), 1)).astype(F32).astype(BF16)
        total = total + jnp.dot(here, q_in[t], preferred_element_type=F32)
    for h in range(heads):
        q_heads[:, h, :] = total[:, h * head_dim:(h + 1) * head_dim]

    for c in k_copies:
        c.wait()
    span = per_req * block_len
    position = lax.broadcasted_iota(jnp.int32, (group, span), 1)
    scale = 1.0 / math.sqrt(head_dim)

    def score_step(i, carry):
        for u in range(4):
            r = i * 4 + u
            limit = len_ref[0, r]
            ids = [table_ref[0, r * per_req + m] for m in range(per_req)]
            for j in range(kv_heads):
                query = q_heads[r, pl.ds(j * group, group), :].astype(BF16)
                keys = jnp.concatenate([k_buf[b, j] for b in ids], axis=0)
                s = lax.dot_general(query, keys, (((1,), (1,)), ((), ())), preferred_element_type=F32) * scale
                score[r, pl.ds(j * group, group), :] = jnp.where(position < limit, s, -1e30)
        return carry

    lax.fori_loop(0, rows // 4, score_step, 0)

    def soft_step(i, carry):
        x = score[pl.ds(i * 4, 4)]
        e = jnp.exp(x - jnp.max(x, axis=2, keepdims=True))
        score[pl.ds(i * 4, 4)] = e / jnp.sum(e, axis=2, keepdims=True)
        return carry

    lax.fori_loop(0, rows // 4, soft_step, 0)

    for c in v_copies:
        c.wait()

    def mix_step(i, carry):
        for u in range(4):
            r = i * 4 + u
            ids = [table_ref[0, r * per_req + m] for m in range(per_req)]
            for j in range(kv_heads):
                weight = score[r, pl.ds(j * group, group), :].astype(BF16)
                values = jnp.concatenate([v_buf[b, j] for b in ids], axis=0)
                mixed[r, pl.ds(j * group, group), :] = jnp.dot(weight, values, preferred_element_type=F32)
        return carry

    lax.fori_loop(0, rows // 4, mix_step, 0)
    for h in range(heads):
        act[:, h * head_dim:(h + 1) * head_dim] = mixed[:, h, :].astype(BF16)

    tile = min(256, chunk)
    rs_copies = []
    for i in range(num_tp):
        w_copies[i].wait()

        def project(n, carry, i=i):
            column = pl.ds(pl.multiple_of(n * tile, tile), tile)
            part = jnp.dot(act[...], w_buf[i, :, column], preferred_element_type=F32)
            if i < num_tp - 1:
                rs_send[i, :, column] = part.astype(BF16)
            else:
                own[:, column] = part
            return carry

        lax.fori_loop(0, chunk // tile, project, 0)
        if i < num_tp - 1:
            c = pltpu.make_async_remote_copy(
                src_ref=rs_send.at[i], dst_ref=rs_in.at[tp], send_sem=rs_ssem.at[i], recv_sem=rs_rsem.at[tp],
                device_id={"tp": tp_peer(i + 1)}, device_id_type=MESH,
            )
            c.start()
            rs_copies.append(c)

    summed = own[...]
    for k in range(1, num_tp):
        src = tp_peer(k)
        pltpu.make_async_remote_copy(
            src_ref=rs_send.at[0], dst_ref=rs_in.at[src], send_sem=rs_ssem.at[0], recv_sem=rs_rsem.at[src],
            device_id={"tp": src}, device_id_type=MESH,
        ).wait_recv()
        summed = summed + rs_in[src].astype(F32)
    gathered[tp] = summed.astype(BF16)

    ag_copies = []
    for k in range(1, num_tp):
        c = pltpu.make_async_remote_copy(
            src_ref=gathered.at[tp], dst_ref=gathered.at[tp], send_sem=ag_ssem.at[k], recv_sem=ag_rsem.at[tp],
            device_id={"tp": tp_peer(k)}, device_id_type=MESH,
        )
        c.start()
        ag_copies.append(c)

    y_copies = []
    for k in range(num_tp):
        src = tp_peer(k)
        if k:
            pltpu.make_async_remote_copy(
                src_ref=gathered.at[src], dst_ref=gathered.at[src], send_sem=ag_ssem.at[k], recv_sem=ag_rsem.at[src],
                device_id={"tp": src}, device_id_type=MESH,
            ).wait_recv()
        column = pl.ds(pl.multiple_of(src * chunk, 128), chunk)
        block = gathered[src]
        for n in list(range(1, num_inst)) + [0]:
            dst = inst_peer(n)
            moved = jnp.dot(place_t[dst].astype(BF16), block, preferred_element_type=F32).astype(BF16)
            if n == 0:
                out_ref[me, :, column] = moved
                continue
            y_send[k, n] = moved
            c = pltpu.make_async_remote_copy(
                src_ref=y_send.at[k, n], dst_ref=out_ref.at[me, :, column],
                send_sem=y_ssem.at[k, n], recv_sem=y_rsem.at[src, me],
                device_id={"inst": dst}, device_id_type=MESH,
            )
            c.start()
            y_copies.append(c)

    for k in range(num_tp):
        piece = tp_peer(k)
        column = pl.ds(pl.multiple_of(piece * chunk, 128), chunk)
        for n in range(1, num_inst):
            src = inst_peer(n)
            pltpu.make_async_remote_copy(
                src_ref=y_send.at[k, n], dst_ref=out_ref.at[src, :, column],
                send_sem=y_ssem.at[k, n], recv_sem=y_rsem.at[piece, src],
                device_id={"inst": src}, device_id_type=MESH,
            ).wait_recv()
    for c in q_copies + rs_copies + ag_copies + y_copies:
        c.wait_send()


def local(queries, k_pool, v_pool, out_weight, lengths, block_table, routes):
    num_inst = lax.axis_size("inst")
    num_tp = lax.axis_size("tp")
    slots, cols = queries.shape
    cap = slots // num_inst
    blocks, kv_heads, block_len, head_dim = k_pool.shape
    rows = routes.shape[0]
    features = out_weight.shape[1]
    chunk = features // num_tp
    heads = cols // head_dim
    span = block_table.shape[1] // rows * block_len
    anywhere = pl.BlockSpec(memory_space=pl.ANY)
    smem = pl.BlockSpec(memory_space=pltpu.SMEM)
    vmem = pl.BlockSpec(memory_space=pltpu.VMEM)
    dma = pltpu.SemaphoreType.DMA
    out = pl.pallas_call(
        functools.partial(kernel, num_inst, num_tp),
        out_shape=jax.ShapeDtypeStruct((num_inst, cap, features), BF16),
        in_specs=[anywhere, anywhere, anywhere, anywhere, smem, smem, vmem],
        out_specs=vmem,
        scratch_shapes=[
            pltpu.VMEM(k_pool.shape, BF16),
            pltpu.VMEM(v_pool.shape, BF16),
            pltpu.VMEM((num_tp, cols, chunk), BF16),
            pltpu.VMEM((num_inst, cap, cols), BF16),
            pltpu.VMEM((rows, heads, head_dim), F32),
            pltpu.VMEM((rows, heads, span), F32),
            pltpu.VMEM((rows, heads, head_dim), F32),
            pltpu.VMEM((rows, cols), BF16),
            pltpu.VMEM((num_inst, cap, rows), F32),
            pltpu.VMEM((num_tp, rows, chunk), BF16),
            pltpu.VMEM((num_tp, rows, chunk), BF16),
            pltpu.VMEM((rows, chunk), F32),
            pltpu.VMEM((num_tp, rows, chunk), BF16),
            pltpu.VMEM((num_tp, num_inst, cap, chunk), BF16),
            dma((PIECES,)),
            dma((PIECES,)),
            dma((num_tp,)),
            dma,
            dma((num_inst,)),
            dma((num_inst,)),
            dma((num_tp,)),
            dma((num_tp,)),
            dma((num_tp,)),
            dma((num_tp,)),
            dma((num_tp, num_inst)),
            dma((num_tp, num_inst)),
        ],
        compiler_params=pltpu.CompilerParams(
            collective_id=0, has_side_effects=True, vmem_limit_bytes=48 * 1024 * 1024
        ),
        cost_estimate=pl.CostEstimate(flops=10**9, bytes_accessed=33 * 10**6, transcendentals=300000),
    )(queries.reshape(num_inst, cap, cols), k_pool, v_pool, out_weight, lengths, block_table, routes)
    return out.reshape(slots, features)


def solution(mesh):
    return jax.shard_map(
        local,
        mesh=mesh,
        in_specs=(
            P(("groups", "inst"), "tp"),
            P(("groups", "inst"), "tp", None, None),
            P(("groups", "inst"), "tp", None, None),
            P("tp", None),
            P(("groups", "inst"), None),
            P(("groups", "inst"), None),
            P(("groups", "inst"), None),
        ),
        out_specs=P(("groups", "inst"), None),
        check_vma=False,
    )
```

time: 116 us -> 44 us (0.38)
  blocking collectives: 54.2 us -> 0 us
  Pallas kernels: 0 us -> 40 us
  matrix products: 24.3 us -> 0 us
  local copies, waits for them, and re-layouts: 28 us -> 3.79 us
  other arithmetic: 4.73 us -> 0 us
  starting transfers between devices: 4.37 us -> 0 us
    psum x1 -> x0, blocking collectives: 44.9 us -> none  [local(): return lax.psum(partial_value, 'tp').astype(jnp.bfloat16)]
    pallas_call x0 -> x1, Pallas kernels: none -> 40 us  [local(): pl.pallas_call(functools.partial(kernel, num_inst, num_tp), out_shape=jax...]
    gather x4 -> x0, local copies, waits for them, and re-layouts: 27.1 us -> none  [the longest x1 12.9 us: local(): value_rows = v_pool[block_ids]]
    dot_general x3 -> x0, matrix products: 24.3 us -> none  [the longest x1 8.8 us: local(): jnp.dot(head_out, out_weight, preferred_element_type=jnp.float32)]
    all_to_all x1 -> x0, blocking collectives: 9.29 us -> none  [local(): lax.all_to_all(source_out.reshape(num_inst, capacity, -1), 'inst', split_...]
    all_to_all x1 -> x0, starting transfers between devices: 4.37 us -> none  [local(): lax.all_to_all(queries.reshape(num_inst, capacity, -1), 'inst', split_axi...]
    unnamed x6 -> x8, local copies, waits for them, and re-layouts: 0.56 us -> 3.79 us
    reduce_sum x3 -> x0, other arithmetic: 1.8 us -> none  [the longest x1 0.87 us: attend(): jnp.sum(scaled, axis=(3, 4), keepdims=True)]
  transfers between devices with their start and end apart: 1 -> 0, of which waited for: 0 -> 0; matrix products, arithmetic and copies ran while one was open for 27% -> 0% of each run, Pallas kernels for 0% -> 0%
where the time goes in v1:
time: 44 us; the launch traced here: 43.8 us
  Pallas kernels  40 us (91%)
  local copies, waits for them, and re-layouts  3.79 us (9%)
    pallas_call x1, Pallas kernels, local(): pl.pallas_call(functools.partial(kernel, num_inst, num_tp), out_shape=jax...  40 us
    unnamed x8, local copies, waits for them, and re-layouts  3.79 us

profile of v1, /device:TPU:0, one launch (start us, length us, event | category | flops | bytes accessed | tf_op | source)
XLA Modules:
  0.0 43.8 jit_solution(6854851103049945003)
XLA Ops:
  0.0 0.7 %copy.8.route_ref = s32[32,1]{1,0:T(8,128)S(1)} copy(s32[32,1]{0,1:T(1,128)} %param.13) | data formatting | bytes 256 | tf_op args[6]
  0.7 0.0 copy-start
  0.7 0.9 %copy-done = bf16[64,2048]{1,0:T(8,128)(2,1)S(1)} copy-done((bf16[64,2048]{1,0:T(8,128)(2,1)S(1)}, bf16[64,2048]{1,0:T(8,128)(2,1)}, u32[]{:S(2)}) %copy-start) | copy-done | bytes 262168
  1.7 0.0 copy-start.1
  1.7 0.7 %copy-done.1 = s32[1,32]{1,0:T(1,128)S(1)} copy-done((s32[1,32]{1,0:T(1,128)S(1)}, s32[1,32]{1,0:T(1,128)}, u32[]{:S(2)}) %copy-start.1) | copy-done | bytes 152
  2.3 0.0 copy-start.2
  2.3 0.7 %copy-done.2 = s32[1,128]{1,0:T(1,128)S(1)} copy-done((s32[1,128]{1,0:T(1,128)S(1)}, s32[1,128]{1,0:T(1,128)}, u32[]{:S(2)}) %copy-start.2) | copy-done | bytes 536
  3.0 40.0 %shard_map.73 = bf16[4,16,4096]{2,1,0:T(8,128)(2,1)S(1)} custom-call(bf16[4,16,2048]{2,1,0:T(8,128)(2,1)S(1)} %bitcast.3, bf16[128,2,128,128]{3,2,1,0:T(8,128)(2,1)} %k_hbm.1, bf16[128,2,128,128]{3,2,1,0:T(8,128)(2,1)} %v_hbm.1, bf16[2048,4096]{1,0:T(8,128)(2,1)} %w_hbm.1, s32[1,32]{1,0:T(1,128)S(1)} %copy-done.1, s32[1,128]{1,0:T(1,128)S(1)} %copy-done.2, ...), custom_call_target="tpu_custom_call" | custom-call | flops 1000000000 | bytes 33000000 | tf_op jit(solution)/shard_map/pallas_call | solution.py:243
  43.1 0.8 %copy.10 = bf16[64,4096]{1,0:T(8,128)(2,1)} copy(bf16[64,4096]{1,0:T(8,128)(2,1)S(1)} %bitcast.2) | data formatting | bytes 1048576
Async XLA Ops:
  0.7 0.9 %copy-start = (bf16[64,2048]{1,0:T(8,128)(2,1)S(1)}, bf16[64,2048]{1,0:T(8,128)(2,1)}, u32[]{:S(2)}) copy-start(bf16[64,2048]{1,0:T(8,128)(2,1)} %param.7) | copy-start | bytes 786436
  1.7 0.7 %copy-start.1 = (s32[1,32]{1,0:T(1,128)S(1)}, s32[1,32]{1,0:T(1,128)}, u32[]{:S(2)}) copy-start(s32[1,32]{1,0:T(1,128)} %len_ref.1) | copy-start | bytes 388
  2.3 0.7 %copy-start.2 = (s32[1,128]{1,0:T(1,128)S(1)}, s32[1,128]{1,0:T(1,128)}, u32[]{:S(2)}) copy-start(s32[1,128]{1,0:T(1,128)} %table_ref.1) | copy-start | bytes 1540

commit v2 on v1

v2 whole, which is shorter than its diff:
```python
import functools
import math

import jax
import jax.numpy as jnp
from jax import lax
from jax.experimental import pallas as pl
from jax.experimental.pallas import tpu as pltpu
from jax.sharding import PartitionSpec as P

MESH = pl.DeviceIdType.MESH
F32 = jnp.float32
BF16 = jnp.bfloat16
PIECES = 4
SUBS = 1
UNROLL = 32


def kernel(
    num_inst, num_tp, q_hbm, k_hbm, v_hbm, w_hbm, len_hbm, table_hbm, route_hbm, out_ref,
    len_ref, table_ref, route_ref, k_buf, v_buf, w_buf, q_in, q_heads, score, mixed, act, place_rows, rs_send, rs_in, own, gathered, y_send,
    int_sem, k_sem, v_sem, w_sem, q_own_sem, q_ssem, q_rsem, rs_ssem, rs_rsem, ag_ssem, ag_rsem, y_ssem, y_rsem,
):
    me = lax.axis_index("inst")
    tp = lax.axis_index("tp")
    blocks, kv_heads, block_len, head_dim = k_buf.shape
    cap = q_in.shape[1]
    cols = q_in.shape[2]
    rows = route_ref.shape[1]
    heads = cols // head_dim
    group = heads // kv_heads
    per_req = table_ref.shape[1] // rows
    sub = w_buf.shape[3]
    chunk = SUBS * sub

    def inst_peer(k):
        return lax.rem(me + k, num_inst)

    def tp_peer(k):
        return lax.rem(tp + k, num_tp)

    size = blocks // PIECES
    k_copies = [
        pltpu.make_async_copy(k_hbm.at[pl.ds(i * size, size)], k_buf.at[pl.ds(i * size, size)], k_sem.at[i])
        for i in range(PIECES)
    ]
    v_copies = [
        pltpu.make_async_copy(v_hbm.at[pl.ds(i * size, size)], v_buf.at[pl.ds(i * size, size)], v_sem.at[i])
        for i in range(PIECES)
    ]
    w_copies = []
    for s in range(SUBS):
        for i in range(num_tp):
            column = pl.multiple_of(tp_peer((i + 1) % num_tp) * chunk + s * sub, 128)
            w_copies.append(
                pltpu.make_async_copy(w_hbm.at[:, pl.ds(column, sub)], w_buf.at[s, i], w_sem.at[s * num_tp + i])
            )
    route_copy = pltpu.make_async_copy(route_hbm, route_ref, int_sem.at[0])
    len_copy = pltpu.make_async_copy(len_hbm, len_ref, int_sem.at[1])
    table_copy = pltpu.make_async_copy(table_hbm, table_ref, int_sem.at[2])
    q_own = pltpu.make_async_copy(q_hbm.at[me], q_in.at[me], q_own_sem)
    for c in [route_copy, len_copy, table_copy, q_own] + k_copies + v_copies + w_copies:
        c.start()

    barrier = pltpu.get_barrier_semaphore()
    for k in range(1, num_inst):
        pl.semaphore_signal(barrier, inc=1, device_id={"inst": inst_peer(k)}, device_id_type=MESH)
    for k in range(1, num_tp):
        pl.semaphore_signal(barrier, inc=1, device_id={"tp": tp_peer(k)}, device_id_type=MESH)
    pl.semaphore_wait(barrier, num_inst + num_tp - 2)

    q_copies = []
    for k in range(1, num_inst):
        peer = inst_peer(k)
        c = pltpu.make_async_remote_copy(
            src_ref=q_hbm.at[peer], dst_ref=q_in.at[me], send_sem=q_ssem.at[k], recv_sem=q_rsem.at[me],
            device_id={"inst": peer}, device_id_type=MESH,
        )
        c.start()
        q_copies.append(c)

    route_copy.wait()
    target = route_ref[...]
    line = lax.broadcasted_iota(jnp.int32, (128, rows), 0)
    onehot = (target == line).astype(F32)
    earlier = (
        lax.broadcasted_iota(jnp.int32, (rows, rows), 0) < lax.broadcasted_iota(jnp.int32, (rows, rows), 1)
    ).astype(F32)
    before = jnp.dot(onehot, earlier, preferred_element_type=F32)
    rank = jnp.sum(before * onehot, axis=0, keepdims=True).astype(jnp.int32)
    turned = (target * cap + rank == line).astype(F32)
    place_rows[...] = turned[:num_inst * cap, :].astype(BF16)
    lane = lax.broadcasted_iota(jnp.int32, (rows, 128), 1).astype(F32)
    slot = jnp.sum(jnp.transpose(turned) * lane, axis=1, keepdims=True).astype(jnp.int32)

    q_own.wait()
    for k in range(1, num_inst):
        src = inst_peer(k)
        pltpu.make_async_remote_copy(
            src_ref=q_hbm.at[src], dst_ref=q_in.at[src], send_sem=q_ssem.at[k], recv_sem=q_rsem.at[src],
            device_id={"inst": src}, device_id_type=MESH,
        ).wait_recv()
    total = jnp.zeros((rows, cols), F32)
    for t in range(num_inst):
        here = (slot - t * cap == lax.broadcasted_iota(jnp.int32, (rows, cap), 1)).astype(F32).astype(BF16)
        total = total + jnp.dot(here, q_in[t], preferred_element_type=F32)
    for h in range(heads):
        q_heads[:, h, :] = total[:, h * head_dim:(h + 1) * head_dim]

    len_copy.wait()
    table_copy.wait()
    for c in k_copies:
        c.wait()
    span = per_req * block_len
    position = lax.broadcasted_iota(jnp.int32, (group, span), 1)
    scale = 1.0 / math.sqrt(head_dim)

    def score_step(i, carry):
        for u in range(UNROLL):
            r = i * UNROLL + u
            limit = len_ref[0, r]
            ids = [table_ref[0, r * per_req + m] for m in range(per_req)]
            for j in range(kv_heads):
                query = q_heads[r, pl.ds(j * group, group), :].astype(BF16)
                keys = jnp.concatenate([k_buf[b, j] for b in ids], axis=0)
                s = lax.dot_general(query, keys, (((1,), (1,)), ((), ())), preferred_element_type=F32) * scale
                score[r, pl.ds(j * group, group), :] = jnp.where(position < limit, s, -1e30)
        return carry

    lax.fori_loop(0, rows // UNROLL, score_step, 0)

    def soft_step(i, carry):
        x = score[pl.ds(i * UNROLL, UNROLL)]
        e = jnp.exp(x - jnp.max(x, axis=2, keepdims=True))
        score[pl.ds(i * UNROLL, UNROLL)] = e * (1.0 / jnp.sum(e, axis=2, keepdims=True))
        return carry

    lax.fori_loop(0, rows // UNROLL, soft_step, 0)

    for c in v_copies:
        c.wait()

    def mix_step(i, carry):
        for u in range(UNROLL):
            r = i * UNROLL + u
            ids = [table_ref[0, r * per_req + m] for m in range(per_req)]
            for j in range(kv_heads):
                weight = score[r, pl.ds(j * group, group), :].astype(BF16)
                values = jnp.concatenate([v_buf[b, j] for b in ids], axis=0)
                mixed[r, pl.ds(j * group, group), :] = jnp.dot(weight, values, preferred_element_type=F32)
        return carry

    lax.fori_loop(0, rows // UNROLL, mix_step, 0)
    for h in range(heads):
        act[:, h * head_dim:(h + 1) * head_dim] = mixed[:, h, :].astype(BF16)

    tile = min(256, sub)
    rs_copies, ag_copies, y_copies = [], [], []
    for s in range(SUBS):
        for i in range(num_tp):
            w_copies[s * num_tp + i].wait()
            for n in range(0, sub, tile):
                part = jnp.dot(act[...], w_buf[s, i, :, n:n + tile], preferred_element_type=F32)
                if i < num_tp - 1:
                    rs_send[s, i, :, n:n + tile] = part.astype(BF16)
                else:
                    own[s, :, n:n + tile] = part
            if i < num_tp - 1:
                c = pltpu.make_async_remote_copy(
                    src_ref=rs_send.at[s, i], dst_ref=rs_in.at[s, tp],
                    send_sem=rs_ssem.at[s, i], recv_sem=rs_rsem.at[s, tp],
                    device_id={"tp": tp_peer(i + 1)}, device_id_type=MESH,
                )
                c.start()
                rs_copies.append(c)

    def columns_of(s, owner):
        return pl.ds(pl.multiple_of(owner * chunk + s * sub, 128), sub)

    def move(s, k):
        owner = tp_peer(k)
        spread = jnp.dot(place_rows[...], gathered[s, owner], preferred_element_type=F32)
        for t in range(num_inst):
            y_send[s, k, t] = spread[t * cap:(t + 1) * cap].astype(BF16)
        for n in list(range(1, num_inst)) + [0]:
            dst = inst_peer(n)
            if n == 0:
                out_ref[me, :, columns_of(s, owner)] = y_send[s, k, me]
                continue
            c = pltpu.make_async_remote_copy(
                src_ref=y_send.at[s, k, dst], dst_ref=out_ref.at[me, :, columns_of(s, owner)],
                send_sem=y_ssem.at[s * num_tp + k, n], recv_sem=y_rsem.at[s * num_tp + owner, me],
                device_id={"inst": dst}, device_id_type=MESH,
            )
            c.start()
            y_copies.append(c)

    for s in range(SUBS):
        summed = own[s]
        for k in range(1, num_tp):
            src = tp_peer(k)
            pltpu.make_async_remote_copy(
                src_ref=rs_send.at[s, 0], dst_ref=rs_in.at[s, src],
                send_sem=rs_ssem.at[s, 0], recv_sem=rs_rsem.at[s, src],
                device_id={"tp": src}, device_id_type=MESH,
            ).wait_recv()
            summed = summed + rs_in[s, src].astype(F32)
        gathered[s, tp] = summed.astype(BF16)
        for k in range(1, num_tp):
            c = pltpu.make_async_remote_copy(
                src_ref=gathered.at[s, tp], dst_ref=gathered.at[s, tp],
                send_sem=ag_ssem.at[s, k], recv_sem=ag_rsem.at[s, tp],
                device_id={"tp": tp_peer(k)}, device_id_type=MESH,
            )
            c.start()
            ag_copies.append(c)
        move(s, 0)

    for s in range(SUBS):
        for k in range(1, num_tp):
            src = tp_peer(k)
            pltpu.make_async_remote_copy(
                src_ref=gathered.at[s, src], dst_ref=gathered.at[s, src],
                send_sem=ag_ssem.at[s, k], recv_sem=ag_rsem.at[s, src],
                device_id={"tp": src}, device_id_type=MESH,
            ).wait_recv()
            move(s, k)

    for s in range(SUBS):
        for k in range(num_tp):
            owner = tp_peer(k)
            for n in range(1, num_inst):
                src = inst_peer(n)
                pltpu.make_async_remote_copy(
                    src_ref=y_send.at[s, k, n], dst_ref=out_ref.at[src, :, columns_of(s, owner)],
                    send_sem=y_ssem.at[s * num_tp + k, n], recv_sem=y_rsem.at[s * num_tp + owner, src],
                    device_id={"inst": src}, device_id_type=MESH,
                ).wait_recv()
    for c in q_copies + rs_copies + ag_copies + y_copies:
        c.wait_send()


def local(queries, k_pool, v_pool, out_weight, lengths, block_table, routes):
    num_inst = lax.axis_size("inst")
    num_tp = lax.axis_size("tp")
    slots, cols = queries.shape
    cap = slots // num_inst
    blocks, kv_heads, block_len, head_dim = k_pool.shape
    rows = routes.shape[0]
    features = out_weight.shape[1]
    sub = features // num_tp // SUBS
    heads = cols // head_dim
    span = block_table.shape[1] // rows * block_len
    hbm = pl.BlockSpec(memory_space=pltpu.HBM)
    vmem = pl.BlockSpec(memory_space=pltpu.VMEM)
    dma = pltpu.SemaphoreType.DMA
    out = pl.pallas_call(
        functools.partial(kernel, num_inst, num_tp),
        out_shape=jax.ShapeDtypeStruct((num_inst, cap, features), BF16),
        in_specs=[hbm] * 7,
        out_specs=vmem,
        scratch_shapes=[
            pltpu.SMEM(lengths.shape, jnp.int32),
            pltpu.SMEM(block_table.shape, jnp.int32),
            pltpu.VMEM((1, rows), jnp.int32),
            pltpu.VMEM(k_pool.shape, BF16),
            pltpu.VMEM(v_pool.shape, BF16),
            pltpu.VMEM((SUBS, num_tp, cols, sub), BF16),
            pltpu.VMEM((num_inst, cap, cols), BF16),
            pltpu.VMEM((rows, heads, head_dim), F32),
            pltpu.VMEM((rows, heads, span), F32),
            pltpu.VMEM((rows, heads, head_dim), F32),
            pltpu.VMEM((rows, cols), BF16),
            pltpu.VMEM((num_inst * cap, rows), BF16),
            pltpu.VMEM((SUBS, num_tp, rows, sub), BF16),
            pltpu.VMEM((SUBS, num_tp, rows, sub), BF16),
            pltpu.VMEM((SUBS, rows, sub), F32),
            pltpu.VMEM((SUBS, num_tp, rows, sub), BF16),
            pltpu.VMEM((SUBS, num_tp, num_inst, cap, sub), BF16),
            dma((3,)),
            dma((PIECES,)),
            dma((PIECES,)),
            dma((SUBS * num_tp,)),
            dma,
            dma((num_inst,)),
            dma((num_inst,)),
            dma((SUBS, num_tp)),
            dma((SUBS, num_tp)),
            dma((SUBS, num_tp)),
            dma((SUBS, num_tp)),
            dma((SUBS * num_tp, num_inst)),
            dma((SUBS * num_tp, num_inst)),
        ],
        compiler_params=pltpu.CompilerParams(
            collective_id=0, has_side_effects=True, vmem_limit_bytes=64 * 1024 * 1024 - 65536
        ),
        cost_estimate=pl.CostEstimate(flops=10**9, bytes_accessed=33 * 10**6, transcendentals=300000),
    )(queries.reshape(num_inst, cap, cols), k_pool, v_pool, out_weight, lengths, block_table, routes.reshape(1, rows))
    return out.reshape(slots, features)


def solution(mesh):
    return jax.shard_map(
        local,
        mesh=mesh,
        in_specs=(
            P(("groups", "inst"), "tp"),
            P(("groups", "inst"), "tp", None, None),
            P(("groups", "inst"), "tp", None, None),
            P("tp", None),
            P(("groups", "inst"), None),
            P(("groups", "inst"), None),
            P(("groups", "inst"), None),
        ),
        out_specs=P(("groups", "inst"), None),
        check_vma=False,
    )
```

time: 44 us -> 37.6 us (0.85)
  Pallas kernels: 40 us -> 35.4 us
  local copies, waits for them, and re-layouts: 3.79 us -> 1.87 us
    pallas_call x1, Pallas kernels: 40 us -> 35.4 us  [local(): pl.pallas_call(functools.partial(kernel, num_inst, num_tp), out_shape=jax...]
    unnamed x8 -> x1, local copies, waits for them, and re-layouts: 3.79 us -> 1.87 us
where the time goes in v2:
time: 37.6 us; the launch traced here: 37.3 us
  Pallas kernels  35.4 us (94%)
  local copies, waits for them, and re-layouts  1.87 us (5%)
    pallas_call x1, Pallas kernels, local(): pl.pallas_call(functools.partial(kernel, num_inst, num_tp), out_shape=jax...  35.4 us
    unnamed x1, local copies, waits for them, and re-layouts  1.87 us

profile of v2, /device:TPU:0, one launch (start us, length us, event | category | flops | bytes accessed | tf_op | source)
XLA Modules:
  0.0 37.3 jit_solution(10501769452694421661)
XLA Ops:
  0.0 35.4 %shard_map.73 = bf16[4,16,4096]{2,1,0:T(8,128)(2,1)} custom-call(bf16[4,16,2048]{2,1,0:T(8,128)(2,1)} %bitcast.4, bf16[128,2,128,128]{3,2,1,0:T(8,128)(2,1)} %k_hbm.1, bf16[128,2,128,128]{3,2,1,0:T(8,128)(2,1)} %v_hbm.1, bf16[2048,4096]{1,0:T(8,128)(2,1)} %w_hbm.1, s32[1,32]{1,0:T(1,128)} %len_hbm.1, s32[1,128]{1,0:T(1,128)} %table_hbm.1, s32[1,32]{1,0:T(1,128)} %bitcast.5), custom_call_target="tpu_custom_call" | custom-call | flops 1000000000 | bytes 33000000 | tf_op jit(solution)/shard_map/pallas_call | solution.py:257
  35.4 1.9 %copy.9 = bf16[64,4096]{1,0:T(8,128)(2,1)} copy(bf16[64,4096]{1,0:T(8,128)(2,1)} %bitcast.3) | data formatting | bytes 1048576

commit v3 on v2

--- a/solution.py
+++ b/solution.py
@@ -59,7 +59,7 @@
     len_copy = pltpu.make_async_copy(len_hbm, len_ref, int_sem.at[1])
     table_copy = pltpu.make_async_copy(table_hbm, table_ref, int_sem.at[2])
     q_own = pltpu.make_async_copy(q_hbm.at[me], q_in.at[me], q_own_sem)
-    for c in [route_copy, len_copy, table_copy, q_own] + k_copies + v_copies + w_copies:
+    for c in [route_copy, len_copy, table_copy, q_own] + k_copies + v_copies:
         c.start()
 
     barrier = pltpu.get_barrier_semaphore()
@@ -111,6 +111,8 @@
     table_copy.wait()
     for c in k_copies:
         c.wait()
+    for c in w_copies:
+        c.start()
     span = per_req * block_len
     position = lax.broadcasted_iota(jnp.int32, (group, span), 1)
     scale = 1.0 / math.sqrt(head_dim)

time: 37.6 us -> 37.3 us (level)
  no operation moved by 1% of the time
where the time goes in v3:
time: 37.3 us; the launch traced here: 37.1 us
  Pallas kernels  35.3 us (95%)
  local copies, waits for them, and re-layouts  1.87 us (5%)
    pallas_call x1, Pallas kernels, local(): pl.pallas_call(functools.partial(kernel, num_inst, num_tp), out_shape=jax...  35.3 us
    unnamed x1, local copies, waits for them, and re-layouts  1.87 us

profile of v3, /device:TPU:0, one launch (start us, length us, event | category | flops | bytes accessed | tf_op | source)
XLA Modules:
  0.0 37.1 jit_solution(12654671067433806878)
XLA Ops:
  0.0 35.3 %shard_map.73 = bf16[4,16,4096]{2,1,0:T(8,128)(2,1)} custom-call(bf16[4,16,2048]{2,1,0:T(8,128)(2,1)} %bitcast.4, bf16[128,2,128,128]{3,2,1,0:T(8,128)(2,1)} %k_hbm.1, bf16[128,2,128,128]{3,2,1,0:T(8,128)(2,1)} %v_hbm.1, bf16[2048,4096]{1,0:T(8,128)(2,1)} %w_hbm.1, s32[1,32]{1,0:T(1,128)} %len_hbm.1, s32[1,128]{1,0:T(1,128)} %table_hbm.1, s32[1,32]{1,0:T(1,128)} %bitcast.5), custom_call_target="tpu_custom_call" | custom-call | flops 1000000000 | bytes 33000000 | tf_op jit(solution)/shard_map/pallas_call | solution.py:259
  35.3 1.9 %copy.9 = bf16[64,4096]{1,0:T(8,128)(2,1)} copy(bf16[64,4096]{1,0:T(8,128)(2,1)} %bitcast.3) | data formatting | bytes 1048576
